TPU v7x, 128 devices: a whole 4x4x4 slice. The times are simulated.
128 devices in a mesh: dp: 4 (over x_hi, core), seq: 32 (over z, y, x_lo).
Axes of the slice: x: 4 (x_hi: 2, x_lo: 2; x = x_hi * 2 + x_lo), y: 4, z: 4, core: 2. Of those that a mesh axis runs over, the one named last changes fastest.
Arguments:
- latent: bfloat16 [4, 16384, 3072], P('dp', 'seq'), may hold values from -6 to 6
- mod_scale: float32 [4, 3072], P('dp'), may hold values from 0.5 to 2
- mod_shift: float32 [4, 3072], P('dp'), may hold values from -4 to 4
- w_query: bfloat16 [3072, 1536], P(('dp', 'seq')), may hold values from -0.109375 to 0.109375
- w_key: bfloat16 [3072, 1536], P(('dp', 'seq')), may hold values from -0.109375 to 0.109375
- w_value: bfloat16 [3072, 1536], P(('dp', 'seq')), may hold values from -0.109375 to 0.109375
- cache_keys: bfloat16 [4, 16384, 1536], P('dp', 'seq'), may hold values from -96 to 96
- cache_values: bfloat16 [4, 16384, 1536], P('dp', 'seq'), may hold values from -6 to 6
- block_lists: int32 [4, 32, 4], P('dp', 'seq'), may hold values from -1 to 31, as said below
Outputs:
- context: bfloat16 [4, 16384, 1536], P('dp', 'seq')
Inputs may be any that keep to these rules, and one draw needn't show every extreme that they name: `block_lists`: each row lists distinct blocks b' of the same clip with |b' - b| <= 2 for its own block b, live entries first, then -1.
All inputs are finite; a program needn't handle non-finite values.
Results may differ from a plain program's by a relative error of at most 0.0065.
The roundings to bfloat16 on the way count: a program that leaves them out, or rounds other values in their place, can miss the bound.
Values may be sent and summed in bfloat16 or wider, within the bound.
No kernel may reach another device: no remote copies, remote signals or barrier semaphores. Data moves between devices by JAX's collectives and lax.ppermute only.
A program may use at most 192 MiB of HBM per device.

v0:
```python
import math

import jax
import jax.numpy as jnp
from jax import lax
from jax.sharding import PartitionSpec as P

HEADS = 12
HS = 128
WIN = 2


def passed_along(value, axis, steps):
    count = lax.axis_size(axis)
    leading, last = (max(0, -steps), min(count, count - steps))
    return lax.ppermute(value, axis, [(source, source + steps) for source in range(leading, last)])


def block_scores(query_heads, key_block, scale_factor):
    rows = key_block.shape[0]
    shaped = key_block.reshape(rows, HEADS, HS)
    return (
        jnp.einsum("qhd,khd->hqk", query_heads, shaped, preferred_element_type=jnp.float32)
        * scale_factor
    )


def weighted_values(weights, value_block):
    rows = value_block.shape[0]
    shaped = value_block.reshape(rows, HEADS, HS)
    return jnp.einsum(
        "hqk,khd->hqd", weights.astype(jnp.bfloat16), shaped, preferred_element_type=jnp.float32
    )


def absorb(query_heads, key_block, value_block, live, scale_factor, state):
    largest, total, summed = state
    scores = jnp.where(live, block_scores(query_heads, key_block, scale_factor), -jnp.inf)
    newest = jnp.maximum(largest, jnp.max(scores, axis=-1))
    rescale = jnp.exp(largest - newest)
    weights = jnp.exp(scores - newest[..., None])
    total = total * rescale + jnp.sum(weights, axis=-1)
    summed = summed * rescale[..., None] + weighted_values(weights, value_block)
    return (newest, total, summed)


def body(
    latent, mod_scale, mod_shift, w_query, w_key, w_value, cache_keys, cache_values, block_lists
):
    values_in = latent[0].astype(jnp.float32)
    factor = lax.rsqrt(jnp.mean(values_in * values_in, axis=-1, keepdims=True) + 1e-06)
    normed = (values_in * factor * mod_scale[0][None, :] + mod_shift[0][None, :]).astype(
        jnp.bfloat16
    )
    rows = normed.shape[0]
    wide = w_query.shape[1]
    pieces = (
        lax.all_gather(w_query, ("dp", "seq"), axis=0, tiled=True),
        lax.all_gather(w_key, ("dp", "seq"), axis=0, tiled=True),
        lax.all_gather(w_value, ("dp", "seq"), axis=0, tiled=True),
    )
    projected = tuple(
        (jnp.dot(normed, piece, preferred_element_type=jnp.float32) for piece in pieces)
    )
    query = projected[0].astype(jnp.bfloat16)
    keys_now = projected[1].astype(jnp.bfloat16)
    values_now = projected[2].astype(jnp.bfloat16)
    block = lax.axis_index("seq")
    listed = block_lists[0, 0]
    key_blocks = []
    value_blocks = []
    flags = []
    for offset in range(-WIN, WIN + 1):
        if offset == 0:
            near_keys, near_values = (cache_keys[0], cache_values[0])
        else:
            near_keys, near_values = passed_along((cache_keys[0], cache_values[0]), "seq", -offset)
        key_blocks.append(near_keys)
        value_blocks.append(near_values)
        flags.append(jnp.any(listed == block + offset))
    scale_factor = 1.0 / math.sqrt(HS)
    query_heads = query.reshape(rows, HEADS, HS)
    first_scores = block_scores(query_heads, keys_now, scale_factor)
    largest = jnp.max(first_scores, axis=-1)
    first_weights = jnp.exp(first_scores - largest[..., None])
    state = (largest, jnp.sum(first_weights, axis=-1), weighted_values(first_weights, values_now))
    for position in range(len(key_blocks)):
        state = absorb(
            query_heads,
            key_blocks[position],
            value_blocks[position],
            flags[position],
            scale_factor,
            state,
        )
    result = state[2] / state[1][..., None]
    return jnp.transpose(result, (1, 0, 2)).reshape(rows, wide).astype(jnp.bfloat16)[None]


def solution(mesh):
    placed = (
        P("dp", "seq", None),
        P("dp", None),
        P("dp", None),
        P(("dp", "seq"), None),
        P(("dp", "seq"), None),
        P(("dp", "seq"), None),
        P("dp", "seq", None),
        P("dp", "seq", None),
        P("dp", "seq", None),
    )
    return jax.shard_map(
        body, mesh=mesh, in_specs=placed, out_specs=P("dp", "seq", None), check_vma=False
    )
```

profile of v0, /device:TPU:64, one launch (start us, length us, event | category | flops | bytes accessed | tf_op | source)
XLA Modules:
  0.0 1127.1 jit_solution(14449335061552771261)
XLA Ops:
  8.7 3.5 collective-permute-start.1
  12.2 3.4 collective-permute-start.3
  15.6 5.5 collective-permute-start.5
  27.6 2.6 copy.49
  33.5 49.5 %collective-permute-done.1 = bf16[512,1536]{1,0:T(8,128)(2,1)} collective-permute-done((bf16[512,1536]{1,0:T(8,128)(2,1)}, bf16[512,1536]{1,0:T(8,128)(2,1)}, u32[]{:S(2)}, u32[]{:S(2)}) %collective-permute-start.1) | collective-permute-done | bytes 1572896 | tf_op jit(solution)/shard_map/ppermute | solution.py:16
  84.9 2.6 copy.40
  87.5 3.9 collective-permute-start.2
  91.4 2.6 copy.44
  94.1 5.7 collective-permute-start
  99.7 2.6 copy.53
  103.9 338.1 %all-gather.4.cloned.1.call-done = bf16[3072,1536]{1,0:T(8,128)(2,1)} async-done(((bf16[24,1536]{1,0:T(8,128)(2,1)}), bf16[3072,1536]{1,0:T(8,128)(2,1)}) %all-gather.4.cloned.1.call-update) | async-done | bytes 9437200 | tf_op jit(solution)/shard_map/all_gather | solution.py:58
  442.1 10.5 convolution_convert_fusion.2
  452.5 304.5 %all-gather.6.cloned.1.call-done = bf16[3072,1536]{1,0:T(8,128)(2,1)} async-done(((bf16[24,1536]{1,0:T(8,128)(2,1)}), bf16[3072,1536]{1,0:T(8,128)(2,1)}) %all-gather.6.cloned.1.call-update) | async-done | bytes 9437200 | tf_op jit(solution)/shard_map/all_gather | solution.py:59
  757.0 10.5 convolution_convert_fusion.1
  769.2 2.8 copy.32
  772.0 7.7 multiply_reduce_fusion
  779.7 8.5 fusion.4
  788.2 3.9 fusion.3
  792.1 3.9 fusion.1
  796.0 8.3 fusion
  804.3 7.2 fusion.2
  811.6 10.0 fusion.29
  821.6 5.0 fusion.27
  826.6 10.0 fusion.25
  836.6 4.9 fusion.23
  841.5 8.9 fusion.7
  850.5 9.3 fusion.11
  859.8 216.4 %all-gather.8.cloned.1.call-done = bf16[3072,1536]{1,0:T(8,128)(2,1)} async-done(((bf16[24,1536]{1,0:T(8,128)(2,1)}), bf16[3072,1536]{1,0:T(8,128)(2,1)}) %all-gather.8.cloned.1.call-update) | async-done | bytes 9437200 | tf_op jit(solution)/shard_map/all_gather | solution.py:60
  1076.2 9.3 convolution_convert_fusion
  1087.2 8.9 fusion.31
  1096.1 12.1 %fusion.5 = (f32[12,512]{1,0:T(8,128)S(1)}, f32[12,512]{1,0:T(8,128)S(1)}) fusion(f32[12,512,512]{1,2,0:T(8,128)} %get-tuple-element.30, f32[12,512]{1,0:T(8,128)S(1)} %get-tuple-element.29, f32[12,512]{1,0:T(8,128)S(1)} %get-tuple-element.16, f32[12,512,512]{1,2,0:T(8,128)} %get-tuple-element.22, pred[]{:T(512)} %get-tuple-element.5), kind=kLoop, calls=%fused_computation.17 | loop fusion | flops 22007808 | bytes 25264128 | tf_op jit(solution)/shard_map/reduce_sum | solution.py:86
  1108.9 8.6 fusion.56
  (57 shorter events, 22.2 us)
Async XLA Ops:
  6.5 23.6 %copy-start.9 = (s32[1,1,4]{2,1,0:T(1,128)S(1)}, s32[1,1,4]{2,1,0:T(1,128)}, u32[]{:S(2)}) copy-start(s32[1,1,4]{2,1,0:T(1,128)} %param.17) | copy-start | bytes 52
  6.5 435.5 %all-gather.4.cloned.1.call-start = ((), (), s32[]{:S(2)}) async-start(), calls=%async_computation | async-start | bytes 9510912 | tf_op jit(solution)/shard_map/all_gather | solution.py:58
  7.3 749.7 %all-gather.6.cloned.1.call-start = ((), (), s32[]{:S(2)}) async-start(), calls=%async_computation.1 | async-start | bytes 9510912 | tf_op jit(solution)/shard_map/all_gather | solution.py:59
  8.0 1068.2 %all-gather.8.cloned.1.call-start = ((), (), s32[]{:S(2)}) async-start(), calls=%async_computation.2 | async-start | bytes 9510912 | tf_op jit(solution)/shard_map/all_gather | solution.py:60
  8.7 74.3 %collective-permute-start.1 = (bf16[512,1536]{1,0:T(8,128)(2,1)}, bf16[512,1536]{1,0:T(8,128)(2,1)}, u32[]{:S(2)}, u32[]{:S(2)}) collective-permute-start(bf16[512,1536]{1,0:T(8,128)(2,1)} %bitcast.172), channel_id=1, source_target_pairs={{0,2},{1,3},{2,4},{3,5},{4,6},{5,7},{6,8},{7,9},{8,10},{9,11},{10,... | collective-permute-start | bytes 4718600 | tf_op jit(solution)/shard_map/ppermute | solution.py:16
  12.2 75.3 %collective-permute-start.3 = (bf16[512,1536]{1,0:T(8,128)(2,1)}, bf16[512,1536]{1,0:T(8,128)(2,1)}, u32[]{:S(2)}, u32[]{:S(2)}) collective-permute-start(bf16[512,1536]{1,0:T(8,128)(2,1)} %bitcast.173), channel_id=1, source_target_pairs={{0,1},{1,2},{2,3},{3,4},{4,5},{5,6},{6,7},{7,8},{8,9},{9,10},{10,1... | collective-permute-start | bytes 4718600 | tf_op jit(solution)/shard_map/ppermute | solution.py:16
  15.6 78.4 %collective-permute-start.5 = (bf16[512,1536]{1,0:T(8,128)(2,1)}, bf16[512,1536]{1,0:T(8,128)(2,1)}, u32[]{:S(2)}, u32[]{:S(2)}) collective-permute-start(bf16[512,1536]{1,0:T(8,128)(2,1)} %bitcast.174), channel_id=1, source_target_pairs={{1,0},{2,1},{3,2},{4,3},{5,4},{6,5},{7,6},{8,7},{9,8},{10,9},{11,1... | collective-permute-start | bytes 4718600 | tf_op jit(solution)/shard_map/ppermute | solution.py:16
  21.1 81.2 %collective-permute-start.7 = (bf16[512,1536]{1,0:T(8,128)(2,1)}, bf16[512,1536]{1,0:T(8,128)(2,1)S(1)}, u32[]{:S(2)}, u32[]{:S(2)}) collective-permute-start(bf16[512,1536]{1,0:T(8,128)(2,1)} %bitcast.175), channel_id=1, source_target_pairs={{2,0},{3,1},{4,2},{5,3},{6,4},{7,5},{8,6},{9,7},{10,8},{11,9},{12,... | collective-permute-start | bytes 4718600 | tf_op jit(solution)/shard_map/ppermute | solution.py:16
  25.2 754.5 %collective-permute-start.6 = (bf16[512,1536]{0,1:T(8,128)(2,1)S(1)}, bf16[512,1536]{0,1:T(8,128)(2,1)}, u32[]{:S(2)}, u32[]{:S(2)}) collective-permute-start(bf16[512,1536]{0,1:T(8,128)(2,1)S(1)} %bitcast.165), channel_id=1, source_target_pairs={{2,0},{3,1},{4,2},{5,3},{6,4},{7,5},{8,6},{9,7},{10,8},{11,9},{12,... | collective-permute-start | bytes 4718600 | tf_op jit(solution)/shard_map/ppermute | solution.py:16
  33.5 408.6 %copy-start.10 = (f32[1,3072]{1,0:T(1,128)S(1)}, f32[1,3072]{1,0:T(1,128)}, u32[]{:S(2)}) copy-start(f32[1,3072]{1,0:T(1,128)} %param.11) | copy-start | bytes 36868
  33.5 408.6 %copy-start.11 = (f32[1,3072]{1,0:T(1,128)S(1)}, f32[1,3072]{1,0:T(1,128)}, u32[]{:S(2)}) copy-start(f32[1,3072]{1,0:T(1,128)} %param.10) | copy-start | bytes 36868
  83.0 705.2 %collective-permute-start.4 = (bf16[512,1536]{0,1:T(8,128)(2,1)S(1)}, bf16[512,1536]{0,1:T(8,128)(2,1)}, u32[]{:S(2)}, u32[]{:S(2)}) collective-permute-start(bf16[512,1536]{0,1:T(8,128)(2,1)S(1)} %bitcast.166), channel_id=1, source_target_pairs={{1,0},{2,1},{3,2},{4,3},{5,4},{6,5},{7,6},{8,7},{9,8},{10,9},{11,1... | collective-permute-start | bytes 4718600 | tf_op jit(solution)/shard_map/ppermute | solution.py:16
  87.5 704.6 %collective-permute-start.2 = (bf16[512,1536]{0,1:T(8,128)(2,1)S(1)}, bf16[512,1536]{0,1:T(8,128)(2,1)}, u32[]{:S(2)}, u32[]{:S(2)}) collective-permute-start(bf16[512,1536]{0,1:T(8,128)(2,1)S(1)} %bitcast.167), channel_id=1, source_target_pairs={{0,1},{1,2},{2,3},{3,4},{4,5},{5,6},{6,7},{7,8},{8,9},{9,10},{10,1... | collective-permute-start | bytes 4718600 | tf_op jit(solution)/shard_map/ppermute | solution.py:16
  94.1 701.9 %collective-permute-start = (bf16[512,1536]{0,1:T(8,128)(2,1)S(1)}, bf16[512,1536]{0,1:T(8,128)(2,1)}, u32[]{:S(2)}, u32[]{:S(2)}) collective-permute-start(bf16[512,1536]{0,1:T(8,128)(2,1)S(1)} %bitcast.168), channel_id=1, source_target_pairs={{0,2},{1,3},{2,4},{3,5},{4,6},{5,7},{6,8},{7,9},{8,10},{9,11},{10,... | collective-permute-start | bytes 4718600 | tf_op jit(solution)/shard_map/ppermute | solution.py:16
  804.3 7.3 copy-start.4
  811.5 15.0 %copy-start.7 = (f32[12,512]{1,0:T(8,128)}, f32[12,512]{1,0:T(8,128)S(1)}, u32[]{:S(2)}) copy-start(f32[12,512]{1,0:T(8,128)S(1)} %get-tuple-element.18) | copy-start | bytes 73732
  811.6 10.0 copy-start.5
  821.6 5.0 copy-start.3
  826.6 10.0 copy-start.6
  841.5 8.9 copy-start.8
  850.5 225.7 %copy-start = (bf16[1,512,3072]{2,1,0:T(8,128)(2,1)S(1)}, bf16[1,512,3072]{2,1,0:T(8,128)(2,1)}, u32[]{:S(2)}) copy-start(bf16[1,512,3072]{2,1,0:T(8,128)(2,1)} %param.9) | copy-start | bytes 9437188
  1087.2 21.7 %slice-start = ((s8[12582912]{0:T(1024)(128)(4,1)}), s8[4194304]{0:T(1024)(128)(4,1)S(1)}, s32[]{:S(2)}) async-start(s8[12582912]{0:T(1024)(128)(4,1)} %bitcast.163), calls=%async_computation.3 | async-start | bytes 8388608
  1087.2 21.7 %slice-start.1 = ((s8[12582912]{0:T(1024)(128)(4,1)}), s8[4194304]{0:T(1024)(128)(4,1)S(1)}, s32[]{:S(2)}) async-start(s8[12582912]{0:T(1024)(128)(4,1)} %bitcast.163), calls=%async_computation.4 | async-start | bytes 8388608
  1096.1 12.8 %slice-start.2 = ((s8[12582912]{0:T(1024)(128)(4,1)}), s8[4194304]{0:T(1024)(128)(4,1)S(1)}, s32[]{:S(2)}) async-start(s8[12582912]{0:T(1024)(128)(4,1)} %bitcast.163), calls=%async_computation.5 | async-start | bytes 8388608
  1096.1 12.8 %copy-start.1 = (f32[12,512,128]{1,2,0:T(8,128)S(1)}, f32[12,512,128]{1,2,0:T(8,128)}, u32[]{:S(2)}) copy-start(f32[12,512,128]{1,2,0:T(8,128)} %fusion.31) | copy-start | bytes 9437188
  1096.1 12.8 %copy-start.2 = (bf16[512,1536]{0,1:T(8,128)(2,1)S(1)}, bf16[512,1536]{0,1:T(8,128)(2,1)}, u32[]{:S(2)}) copy-start(bf16[512,1536]{0,1:T(8,128)(2,1)} %copy.57) | copy-start | bytes 4718596
Sparse Core Ops, SparseCore 0:
  9.1 432.9 all-gather.3
  443.8 313.1 all-gather.5
  758.7 317.4 all-gather.7
where the time goes:
time: 1140 us; the launch traced here: 1130 us
  waiting for transfers between devices  911 us (80%)
  matrix products  117 us (10%)
  other arithmetic  34.3 us (3%)
  starting transfers between devices  28.7 us (3%)
  local copies, waits for them, and re-layouts  22.5 us (2%)
  between operations  13.8 us (1%)
    all_gather x1, waiting for transfers between devices, body(): lax.all_gather(w_query, ('dp', 'seq'), axis=0, tiled=True)  338 us
    all_gather x1, waiting for transfers between devices, body(): lax.all_gather(w_key, ('dp', 'seq'), axis=0, tiled=True)  304 us
    all_gather x1, waiting for transfers between devices, body(): lax.all_gather(w_value, ('dp', 'seq'), axis=0, tiled=True)  216 us
    ppermute x8, waiting for transfers between devices, passed_along(): lax.ppermute(value, axis, [(source, source + steps) for source in range(l...  49.5 us
    dot_general x6, matrix products, weighted_values(): jnp.einsum('hqk,khd->hqd', weights.astype(jnp.bfloat16), shaped, preferre...  47.5 us
    dot_general x6, matrix products, block_scores(): jnp.einsum('qhd,khd->hqk', query_heads, shaped, preferred_element_type=jn...  39.5 us
    dot_general x3, matrix products, body(): jnp.dot(normed, piece, preferred_element_type=jnp.float32)  30.2 us
    ppermute x8, starting transfers between devices, passed_along(): lax.ppermute(value, axis, [(source, source + steps) for source in range(l...  28.6 us
  transfers between devices with their start and end apart: 11, of which 4 were waited for; matrix products, arithmetic and copies ran while one was open for 12% of the time, Pallas kernels for 0%

commit v1 on v0

v1 whole, which is shorter than its diff:
```python
import functools
import itertools
import math

import jax
import jax.numpy as jnp
from jax import lax
from jax.experimental import pallas as pl
from jax.experimental.pallas import tpu as pltpu
from jax.sharding import Mesh
from jax.sharding import PartitionSpec as P

HEADS = 12
HS = 128
NX, NZ, NY = 2, 4, 4
AXES = ("xh", "c", "z", "y", "xl")
DIMS = (2, 2, 4, 4, 2)
BF = jnp.bfloat16
F32 = jnp.float32
HALF = HEADS // 2


def flat(place):
    index = 0
    for at, size in zip(place, DIMS):
        index = index * size + at
    return index


def permuted(value, move):
    places = itertools.product(*(range(n) for n in DIMS))
    moves = ((place, move(*place)) for place in places)
    return lax.ppermute(value, AXES, [(flat(p), flat(q)) for p, q in moves if q is not None])


def other_core(xh, c, z, y, xl):
    return xh, 1 - c, z, y, xl


def along_z(step):
    return lambda xh, c, z, y, xl: (xh, c, (z + step) % NZ, y, xl)


def along_x(xh, c, z, y, xl):
    return xh, c, z, y, 1 - xl


def along_blocks(step):
    def move(xh, c, z, y, xl):
        at = z * NY + y + step
        return (xh, c, at // NY, at % NY, xl) if 0 <= at < NZ * NY else None

    return move


def diagonal(xh, c, z, y, xl):
    return along_blocks(1 if xl == 0 else -1)(xh, c, z, y, xl)


def project_kernel(z_ref, mine_ref, other_ref, w0, wb, wa, wt, wu, mine_out, other_out):
    z = z_ref[0]
    depth = wt.shape[0]
    for src, dst in ((mine_ref, mine_out), (other_ref, other_out)):
        acc = jnp.dot(src[z], w0[...], preferred_element_type=F32)
        acc += jnp.dot(src[(z + 3) % 4], wb[...], preferred_element_type=F32)
        acc += jnp.dot(src[(z + 1) % 4], wa[...], preferred_element_type=F32)
        far = src.at[(z + 2) % 4]
        acc += jnp.dot(far[:, :depth], wt[...], preferred_element_type=F32)
        acc += jnp.dot(far[:, depth:], wu[...], preferred_element_type=F32)
        dst[...] = acc.astype(BF)


def project(z, mine, other, pieces):
    rows, depth = mine.shape[1:]
    wide = pieces[0].shape[1]
    tile = 256
    whole = [pl.BlockSpec(p.shape, lambda i, z_ref: (0, 0)) for p in pieces]
    source = pl.BlockSpec((4, tile, depth), lambda i, z_ref: (0, i, 0))
    target = pl.BlockSpec((tile, wide), lambda i, z_ref: (i, 0))
    return pl.pallas_call(
        project_kernel,
        grid_spec=pltpu.PrefetchScalarGridSpec(
            num_scalar_prefetch=1,
            grid=(rows // tile,),
            in_specs=[source, source, *whole],
            out_specs=[target, target],
        ),
        out_shape=[jax.ShapeDtypeStruct((rows, wide), BF)] * 2,
        compiler_params=pltpu.CompilerParams(vmem_limit_bytes=48 << 20),
        cost_estimate=pl.CostEstimate(
            flops=2 * 2 * rows * 4 * depth * wide,
            bytes_accessed=2 * 2 * rows * (4 * depth + wide) + 8 * depth * wide,
            transcendentals=0,
        ),
    )(z, mine, other, *pieces)


def attend_kernel(flags, *refs):
    queries, keys, values = refs[0:2], refs[2:4], refs[4:6]
    cached_keys, cached_values = refs[6:16], refs[16:26]
    outs = refs[26:28]
    tops, sums, accs = refs[28:31]
    factor = math.log2(math.e) / math.sqrt(HS)

    def scores(half, key):
        return (
            lax.dot_general(
                queries[half][...], key[...], (((1,), (1,)), ((), ())), preferred_element_type=F32
            )
            * factor
        )

    for half in range(2):
        s = scores(half, keys[half])
        top = jnp.max(s, axis=-1, keepdims=True)
        p = jnp.exp2(s - top)
        tops[half] = jnp.broadcast_to(top, tops.shape[1:])
        sums[half] = jnp.broadcast_to(jnp.sum(p, axis=-1, keepdims=True), sums.shape[1:])
        accs[half] = jnp.dot(p.astype(BF), values[half][...], preferred_element_type=F32)
    for n in range(5):

        @pl.when(flags[n] > 0)
        def _():
            for half in range(2):
                s = scores(half, cached_keys[2 * n + half])
                old = tops[half][:, :1]
                top = jnp.maximum(old, jnp.max(s, axis=-1, keepdims=True))
                p = jnp.exp2(s - top)
                scale = jnp.exp2(old - top)
                tops[half] = jnp.broadcast_to(top, tops.shape[1:])
                total = sums[half][:, :1] * scale + jnp.sum(p, axis=-1, keepdims=True)
                sums[half] = jnp.broadcast_to(total, sums.shape[1:])
                accs[half] = accs[half] * scale + jnp.dot(
                    p.astype(BF), cached_values[2 * n + half][...], preferred_element_type=F32
                )

    for half in range(2):
        outs[half][...] = (accs[half] / sums[half][:, :1]).astype(BF)


def attend(flags, queries, keys, values, cached_keys, cached_values):
    rows = queries[0].shape[0]
    near = pl.BlockSpec((rows, HS), lambda g, flags: (0, g))
    halves = [
        pl.BlockSpec((rows, HS), lambda g, flags: (0, flags[5] * HALF + g)),
        pl.BlockSpec((rows, HS), lambda g, flags: (0, (1 - flags[5]) * HALF + g)),
    ]
    twice = lambda arrays: [a for a in arrays for _ in range(2)]
    out = jax.ShapeDtypeStruct((rows, HALF * HS), BF)
    return pl.pallas_call(
        attend_kernel,
        grid_spec=pltpu.PrefetchScalarGridSpec(
            num_scalar_prefetch=1,
            grid=(HALF,),
            in_specs=[near] * 6 + halves * 10,
            out_specs=[near, near],
            scratch_shapes=[
                pltpu.VMEM((2, rows, HS), F32),
                pltpu.VMEM((2, rows, HS), F32),
                pltpu.VMEM((2, rows, HS), F32),
            ],
        ),
        out_shape=[out, out],
        compiler_params=pltpu.CompilerParams(vmem_limit_bytes=48 << 20),
        cost_estimate=pl.CostEstimate(
            flops=6 * 4 * rows * rows * HEADS * HS,
            bytes_accessed=14 * 2 * rows * HEADS * HS,
            transcendentals=6 * rows * rows * HEADS,
        ),
    )(flags, *queries, *keys, *values, *twice(cached_keys), *twice(cached_values))


def body(
    latent, mod_scale, mod_shift, w_query, w_key, w_value, cache_keys, cache_values, block_lists
):
    core = lax.axis_index("c")
    z, y, xl = lax.axis_index("z"), lax.axis_index("y"), lax.axis_index("xl")
    own_keys, own_values = cache_keys[0], cache_values[0]
    rows = latent.shape[1]

    stacked = jnp.concatenate([w_query, w_key, w_value], axis=0)
    left, right = stacked[:, : HALF * HS], stacked[:, HALF * HS :]
    first = core == 0
    kept, sent = jnp.where(first, left, right), jnp.where(first, right, left)
    got = permuted(sent, other_core)
    thin = w_query.shape[0]
    shape = (3, 1, thin, HALF * HS)
    kept, got = kept.reshape(shape), got.reshape(shape)
    pair = jnp.concatenate([jnp.where(first, kept, got), jnp.where(first, got, kept)], axis=1)
    ring = lax.all_gather(pair.reshape(3, 2 * thin, HALF * HS), ("xh", "xl"), axis=0, tiled=False)
    plane = lax.all_gather(ring, "y", axis=0, tiled=False)
    plane = jnp.moveaxis(plane.reshape(16, 3, 2 * thin, HALF * HS), 1, 0)
    plane = plane.reshape(3, 16 * 2 * thin, HALF * HS)

    values_in = latent[0].astype(F32)
    factor = lax.rsqrt(jnp.mean(values_in * values_in, axis=-1, keepdims=True) + 1e-06)
    normed = (values_in * factor * mod_scale[0][None, :] + mod_shift[0][None, :]).astype(BF)
    depth = 16 * 2 * thin
    by_z = jnp.transpose(normed.reshape(rows, 4, 4, depth // 4), (2, 0, 1, 3)).reshape(4, rows, depth)
    place = lax.broadcasted_iota(jnp.int32, (depth, depth), 1)
    row = place % thin
    at_c = place // thin % 2
    at_xl = place // (2 * thin) % 2
    at_xh = place // (4 * thin) % 2
    at_y = place // (8 * thin)
    wanted = (((at_xh * 2 + at_c) * 4 + at_y) * 2 + at_xl) * thin + row
    order = (lax.broadcasted_iota(jnp.int32, (depth, depth), 0) == wanted).astype(BF)
    mine = lax.dot_general(by_z, order, (((2,), (0,)), ((), ())), preferred_element_type=BF)
    other = permuted(mine, other_core)

    x_keys, x_values = permuted(own_keys, along_x), permuted(own_values, along_x)
    before_values = permuted(own_values, along_blocks(1))
    after_values = permuted(own_values, along_blocks(-1))
    before_keys = permuted(own_keys, along_blocks(1))
    after_keys = permuted(own_keys, along_blocks(-1))
    far_values = permuted(jnp.where(xl == 1, before_values, after_values), along_x)
    far_keys = permuted(x_keys, diagonal)

    block = (z * NY + y) * 2 + xl
    listed = block_lists[0, 0]
    side = jnp.where(xl == 0, 1, -1)
    offsets = (0 * side, side, 0 * side - 2, 0 * side + 2, -side)
    flags = [jnp.any(listed == block + offset).astype(jnp.int32) for offset in offsets]
    flags = jnp.stack([*flags, core.astype(jnp.int32)])

    z_index = z.astype(jnp.int32)[None]
    results = []
    for n in range(3):
        piece = plane[n]
        below = permuted(piece, along_z(1))
        above = permuted(piece, along_z(-1))
        top = permuted(below[: depth // 2], along_z(1))
        bottom = permuted(above[depth // 2 :], along_z(-1))
        own, theirs = project(z_index, mine, other, (piece, below, above, top, bottom))
        results.append((own, permuted(theirs, other_core)))

    context = attend(
        flags,
        *results,
        (own_keys, x_keys, before_keys, after_keys, far_keys),
        (own_values, x_values, before_values, after_values, far_values),
    )
    low = jnp.where(first, context[0], context[1])
    high = jnp.where(first, context[1], context[0])
    return jnp.concatenate([low, high], axis=1)[None]


def solution(mesh):
    fine = Mesh(mesh.devices.reshape(DIMS), AXES)
    dp, seq = ("xh", "c"), ("z", "y", "xl")
    placed = (
        P(dp, seq, None),
        P(dp, None),
        P(dp, None),
        P(dp + seq, None),
        P(dp + seq, None),
        P(dp + seq, None),
        P(dp, seq, None),
        P(dp, seq, None),
        P(dp, seq, None),
    )
    return jax.shard_map(
        body, mesh=fine, in_specs=placed, out_specs=P(dp, seq, None), check_vma=False
    )
```

time: 1140 us -> 420 us (0.37)
  waiting for transfers between devices: 911 us -> 169 us
  Pallas kernels: 0 us -> 115 us
  matrix products: 117 us -> 5.01 us
  starting transfers between devices: 28.7 us -> 64.6 us
  other arithmetic: 34.3 us -> 10.3 us
  blocking collectives: 0 us -> 15 us
    all_gather x3 -> x1, waiting for transfers between devices: 859 us -> 51.4 us  [body(): plane = lax.all_gather(ring, 'y', axis=0, tiled=False)]
    pallas_call x0 -> x4, Pallas kernels: none -> 115 us  [the longest x1 88.2 us: attend(): pl.pallas_call(attend_kernel, grid_spec=pltpu.PrefetchScalarGridSpec(num_...]
    dot_general x15 -> x1, matrix products: 117 us -> 5.01 us  [body(): lax.dot_general(by_z, order, (((2,), (0,)), ((), ())), preferred_element_...]
    ppermute x8 -> x25, waiting for transfers between devices: 49.5 us -> 117 us  [permuted(): lax.ppermute(value, AXES, [(flat(p), flat(q)) for p, q in moves if q is n...]
    ppermute x8 -> x25, starting transfers between devices: 28.6 us -> 64.6 us  [permuted(): lax.ppermute(value, AXES, [(flat(p), flat(q)) for p, q in moves if q is n...]
    reduce_sum x3 -> x0, other arithmetic: 30.3 us -> none  [the longest x2 18.2 us: absorb(): total = total * rescale + jnp.sum(weights, axis=-1)]
    all_gather x0 -> x1, blocking collectives: none -> 15 us  [body(): lax.all_gather(pair.reshape(3, 2 * thin, HALF * HS), ('xh', 'xl'), axis=0...]
  transfers between devices with their start and end apart: 11 -> 26, of which waited for: 4 -> 11; matrix products, arithmetic and copies ran while one was open for 12% -> 7% of each run, Pallas kernels for 0% -> 6%
where the time goes in v1:
time: 420 us; the launch traced here: 418 us
  waiting for transfers between devices  169 us (40%)
  Pallas kernels  115 us (27%)
  starting transfers between devices  64.6 us (15%)
  local copies, waits for them, and re-layouts  23.2 us (6%)
  between operations  16.9 us (4%)
  blocking collectives  15 us (4%)
  other arithmetic  10.3 us (2%)
  matrix products  5.01 us (1%)
    ppermute x25, waiting for transfers between devices, permuted(): lax.ppermute(value, AXES, [(flat(p), flat(q)) for p, q in moves if q is n...  117 us
    pallas_call x1, Pallas kernels, attend(): pl.pallas_call(attend_kernel, grid_spec=pltpu.PrefetchScalarGridSpec(num_...  88.2 us
    ppermute x25, starting transfers between devices, permuted(): lax.ppermute(value, AXES, [(flat(p), flat(q)) for p, q in moves if q is n...  64.6 us
    all_gather x1, waiting for transfers between devices, body(): plane = lax.all_gather(ring, 'y', axis=0, tiled=False)  51.4 us
    pallas_call x3, Pallas kernels, project(): pl.pallas_call(project_kernel, grid_spec=pltpu.PrefetchScalarGridSpec(num...  26.6 us
    all_gather x1, blocking collectives, body(): lax.all_gather(pair.reshape(3, 2 * thin, HALF * HS), ('xh', 'xl'), axis=0...  15 us
    unnamed x70, local copies, waits for them, and re-layouts  11.8 us
  transfers between devices with their start and end apart: 26, of which 11 were waited for; matrix products, arithmetic and copies ran while one was open for 7% of the time, Pallas kernels for 6%

profile of v1, /device:TPU:64, one launch (start us, length us, event | category | flops | bytes accessed | tf_op | source)
XLA Modules:
  0.0 418.5 jit_solution(16437122401270453677)
XLA Ops:
  9.3 1.3 collective-permute-done.1
  10.7 15.0 %all_gather.9 = bf16[4,3,48,768]{3,2,0,1:T(8,128)(2,1)} all-gather(bf16[1,3,48,768]{3,2,0,1:T(8,128)(2,1)S(1)} %bitcast.44), channel_id=1, replica_groups=mesh['xh'=2,'c'=2,'z'=4,'y'=4,'xl'=2] {'xh','xl'}, dimensions={0}, use_global_device_ids=true | all-gather | bytes 1105920 | tf_op jit(solution)/shard_map/all_gather | solution.py:190
  25.7 3.5 collective-permute-start.22
  29.2 3.2 copy.12
  36.3 2.0 copy.13
  41.8 51.4 %all-gather.3.cloned.1.call-done = bf16[16,3,48,768]{3,2,0,1:T(8,128)(2,1)} async-done(((bf16[4,3,48,768]{3,2,0,1:T(8,128)(2,1)}), bf16[16,3,48,768]{3,2,0,1:T(8,128)(2,1)}) %all-gather.3.cloned.1.call-update) | async-done | bytes 3538960 | tf_op jit(solution)/shard_map/all_gather | solution.py:191
  93.3 2.4 fusion.61
  95.8 2.0 collective-permute-start.13
  97.9 5.0 %fusion.13.mine_ref = bf16[4,512,768]{2,1,0:T(8,128)(2,1)} fusion(bf16[4,512,768]{1,2,0:T(8,128)(2,1)S(1)} %bitcast.43, s32[768]{0:T(1024)S(1)} %get-tuple-element.36, s32[768]{0:T(1024)S(1)} %copy-done.22, s32[768]{0:T(1024)S(1)} %get-tuple-element.33, s32[768]{0:T(1024)S(1)} %copy-done.23, s32[768]{0:T(1024)S(1)} %get-tuple-element.34, ...), kind=kOutput, calls=%fused_computation.30 | convolution fusion | flops 2443640832 | bytes 6326016 | tf_op jit(solution)/shard_map/dot_general | solution.py:208
  103.3 1.6 collective-permute-start.7
  104.9 19.6 %collective-permute-done.12.wb = bf16[768,768]{1,0:T(8,128)(2,1)S(1)} collective-permute-done((bf16[768,768]{1,0:T(8,128)(2,1)S(1)}, bf16[768,768]{1,0:T(8,128)(2,1)S(1)}, u32[]{:S(2)}, u32[]{:S(2)}) %collective-permute-start.12) | collective-permute-done | bytes 1179680 | tf_op jit(solution)/shard_map/ppermute | solution.py:33
  124.6 2.2 collective-permute-start.23
  127.6 21.4 %collective-permute-done.8.wa = bf16[768,768]{1,0:T(8,128)(2,1)S(1)} collective-permute-done((bf16[768,768]{1,0:T(8,128)(2,1)S(1)}, bf16[768,768]{1,0:T(8,128)(2,1)S(1)}, u32[]{:S(2)}, u32[]{:S(2)}) %collective-permute-start.8) | collective-permute-done | bytes 1179680 | tf_op jit(solution)/shard_map/ppermute | solution.py:33
  149.0 2.0 collective-permute-start.2
  154.6 6.7 %collective-permute-done.23.refs_22_.refs_23_ = bf16[512,1536]{1,0:T(8,128)(2,1)S(1)} collective-permute-done((bf16[512,1536]{1,0:T(8,128)(2,1)}, bf16[512,1536]{1,0:T(8,128)(2,1)S(1)}, u32[]{:S(2)}, u32[]{:S(2)}) %collective-permute-start.23) | collective-permute-done | bytes 1572896 | tf_op jit(solution)/shard_map/ppermute | solution.py:33
  161.9 2.1 collective-permute-start.15
  164.0 13.9 %collective-permute-done.2.wb = bf16[768,768]{1,0:T(8,128)(2,1)S(1)} collective-permute-done((bf16[768,768]{1,0:T(8,128)(2,1)S(1)}, bf16[768,768]{1,0:T(8,128)(2,1)S(1)}, u32[]{:S(2)}, u32[]{:S(2)}) %collective-permute-start.2) | collective-permute-done | bytes 1179680 | tf_op jit(solution)/shard_map/ppermute | solution.py:33
  177.9 1.7 collective-permute-start.10
  180.9 1.9 collective-permute-start.9
  185.2 2.1 collective-permute-start.18
  187.3 3.4 collective-permute-done.14.wt
  190.7 37.4 %collective-permute-start.19 = (bf16[512,1536]{1,0:T(8,128)(2,1)}, bf16[512,1536]{1,0:T(8,128)(2,1)S(1)}, u32[]{:S(2)}, u32[]{:S(2)}) collective-permute-start(bf16[512,1536]{1,0:T(8,128)(2,1)} %bitcast.38), channel_id=1, source_target_pairs={{2,0},{3,1},{4,2},{5,3},{6,4},{7,5},{8,6},{9,7},{10,8},{11,9},{12,... | collective-permute-start | bytes 4718600 | tf_op jit(solution)/shard_map/ppermute | solution.py:33
  229.0 1.6 collective-permute-start.4
  231.0 1.3 broadcast_select_fusion
  232.4 9.0 %shard_map.93 = (bf16[512,768]{1,0:T(8,128)(2,1)S(1)}, bf16[512,768]{1,0:T(8,128)(2,1)}) custom-call(s32[1]{0:T(128)} %bitcast.6.z_ref, bf16[4,512,768]{2,1,0:T(8,128)(2,1)} %fusion.13.mine_ref, bf16[4,512,768]{2,1,0:T(8,128)(2,1)} %collective-permute-done.other_ref, bf16[768,768]{1,0:T(8,128)(2,1)S(1)} %bitcast.35, bf16[768,768]{1,0:T(8,128)(2,1)S(1)} %copy-done.5, ...), custom_call_target="tpu_custom_call" | custom-call | flops 4831838208 | bytes 12582912 | tf_op jit(solution)/shard_map/pallas_call | solution.py:80
  242.3 22.2 %collective-permute-done.4.wt = bf16[384,768]{1,0:T(8,128)(2,1)S(1)} collective-permute-done((bf16[384,768]{1,0:T(8,128)(2,1)S(1)}, bf16[384,768]{1,0:T(8,128)(2,1)S(1)}, u32[]{:S(2)}, u32[]{:S(2)}) %collective-permute-start.4) | collective-permute-done | bytes 589856 | tf_op jit(solution)/shard_map/ppermute | solution.py:33
  265.3 1.9 collective-permute-start.20
  267.2 8.9 %shard_map.92 = (bf16[512,768]{1,0:T(8,128)(2,1)S(1)}, bf16[512,768]{1,0:T(8,128)(2,1)}) custom-call(s32[1]{0:T(128)} %bitcast.6.z_ref, bf16[4,512,768]{2,1,0:T(8,128)(2,1)} %fusion.13.mine_ref, bf16[4,512,768]{2,1,0:T(8,128)(2,1)} %collective-permute-done.other_ref, bf16[768,768]{1,0:T(8,128)(2,1)S(1)} %bitcast.32, bf16[768,768]{1,0:T(8,128)(2,1)S(1)} %copy-done.7, ...), custom_call_target="tpu_custom_call" | custom-call | flops 4831838208 | bytes 12582912 | tf_op jit(solution)/shard_map/pallas_call | solution.py:80
  276.1 8.7 %shard_map.91 = (bf16[512,768]{1,0:T(8,128)(2,1)S(1)}, bf16[512,768]{1,0:T(8,128)(2,1)}) custom-call(s32[1]{0:T(128)} %bitcast.6.z_ref, bf16[4,512,768]{2,1,0:T(8,128)(2,1)} %fusion.13.mine_ref, bf16[4,512,768]{2,1,0:T(8,128)(2,1)} %collective-permute-done.other_ref, bf16[768,768]{1,0:T(8,128)(2,1)S(1)} %bitcast.29, bf16[768,768]{1,0:T(8,128)(2,1)S(1)} %copy-done.9, ...), custom_call_target="tpu_custom_call" | custom-call | flops 4831838208 | bytes 12582912 | tf_op jit(solution)/shard_map/pallas_call | solution.py:80
  292.4 8.7 %collective-permute-done.24.refs_24_.refs_25_ = bf16[512,1536]{1,0:T(8,128)(2,1)} collective-permute-done((bf16[512,1536]{1,0:T(8,128)(2,1)}, bf16[512,1536]{1,0:T(8,128)(2,1)}, u32[]{:S(2)}, u32[]{:S(2)}) %collective-permute-start.24) | collective-permute-done | bytes 1572896 | tf_op jit(solution)/shard_map/ppermute | solution.py:33
  301.1 19.8 %collective-permute-done.20.refs_14_.refs_15_ = bf16[512,1536]{1,0:T(8,128)(2,1)} collective-permute-done((bf16[512,1536]{1,0:T(8,128)(2,1)}, bf16[512,1536]{1,0:T(8,128)(2,1)}, u32[]{:S(2)}, u32[]{:S(2)}) %collective-permute-start.20) | collective-permute-done | bytes 1572896 | tf_op jit(solution)/shard_map/ppermute | solution.py:33
  322.0 88.2 %shard_map.94 = (bf16[512,768]{1,0:T(8,128)(2,1)S(1)}, bf16[512,768]{1,0:T(8,128)(2,1)S(1)}) custom-call(s32[6]{0:T(128)S(1)} %stack.47.flags, bf16[512,768]{1,0:T(8,128)(2,1)S(1)} %copy-done.3, bf16[512,768]{1,0:T(8,128)(2,1)} %collective-permute-done.6.refs_1_, bf16[512,768]{1,0:T(8,128)(2,1)S(1)} %get-tuple-element.15.refs_2_, ...), custom_call_target="tpu_custom_call" | custom-call | flops 9663676416 | bytes 22020096 | tf_op jit(solution)/shard_map/pallas_call | solution.py:150
  (130 shorter events, 29.5 us)
Async XLA Ops:
  6.5 86.7 %all-gather.3.cloned.1.call-start = ((), (), s32[]{:S(2)}) async-start(), calls=%async_computation | async-start | bytes 4423680 | tf_op jit(solution)/shard_map/all_gather | solution.py:191
  9.2 1.4 collective-permute-start.1
  25.7 77.6 %collective-permute-start.22 = (bf16[512,1536]{1,0:T(8,128)(2,1)}, bf16[512,1536]{1,0:T(8,128)(2,1)}, u32[]{:S(2)}, u32[]{:S(2)}) collective-permute-start(bf16[512,1536]{1,0:T(8,128)(2,1)} %bitcast.19.refs_16_.refs_17_), channel_id=1, source_target_pairs={{0,2},{1,3},{2,4},{3,5},{4,6},{5,7},{6,8},{7,9},{8,10},{9,11},{10,... | collective-permute-start | bytes 4718600 | tf_op jit(solution)/shard_map/ppermute | solution.py:33
  95.7 28.9 %collective-permute-start.12 = (bf16[768,768]{1,0:T(8,128)(2,1)S(1)}, bf16[768,768]{1,0:T(8,128)(2,1)S(1)}, u32[]{:S(2)}, u32[]{:S(2)}) collective-permute-start(bf16[768,768]{1,0:T(8,128)(2,1)S(1)} %bitcast.33), channel_id=1, source_target_pairs={{0,8},{1,9},{2,10},{3,11},{4,12},{5,13},{6,14},{7,15},{8,16},{9,17... | collective-permute-start | bytes 3538952 | tf_op jit(solution)/shard_map/ppermute | solution.py:33
  95.8 31.0 %collective-permute-start.13 = (bf16[768,768]{1,0:T(8,128)(2,1)S(1)}, bf16[768,768]{1,0:T(8,128)(2,1)S(1)}, u32[]{:S(2)}, u32[]{:S(2)}) collective-permute-start(bf16[768,768]{1,0:T(8,128)(2,1)S(1)} %bitcast.34), channel_id=1, source_target_pairs={{0,24},{1,25},{2,26},{3,27},{4,28},{5,29},{6,30},{7,31},{8,0},{9,1... | collective-permute-start | bytes 3538952 | tf_op jit(solution)/shard_map/ppermute | solution.py:33
  102.9 82.3 %collective-permute-start = (bf16[4,512,768]{2,1,0:T(8,128)(2,1)}, bf16[4,512,768]{2,1,0:T(8,128)(2,1)}, u32[]{:S(2)}, u32[]{:S(2)}) collective-permute-start(bf16[4,512,768]{2,1,0:T(8,128)(2,1)} %fusion.13.mine_ref), channel_id=1, source_target_pairs={{0,32},{1,33},{2,34},{3,35},{4,36},{5,37},{6,38},{7,39},{8,40},{9,... | collective-permute-start | bytes 9437192 | tf_op jit(solution)/shard_map/ppermute | solution.py:33
  102.9 46.1 %collective-permute-start.8 = (bf16[768,768]{1,0:T(8,128)(2,1)S(1)}, bf16[768,768]{1,0:T(8,128)(2,1)S(1)}, u32[]{:S(2)}, u32[]{:S(2)}) collective-permute-start(bf16[768,768]{1,0:T(8,128)(2,1)S(1)} %bitcast.30), channel_id=1, source_target_pairs={{0,24},{1,25},{2,26},{3,27},{4,28},{5,29},{6,30},{7,31},{8,0},{9,1... | collective-permute-start | bytes 3538952 | tf_op jit(solution)/shard_map/ppermute | solution.py:33
  103.3 47.7 %collective-permute-start.7 = (bf16[768,768]{1,0:T(8,128)(2,1)S(1)}, bf16[768,768]{1,0:T(8,128)(2,1)S(1)}, u32[]{:S(2)}, u32[]{:S(2)}) collective-permute-start(bf16[768,768]{1,0:T(8,128)(2,1)S(1)} %bitcast.31), channel_id=1, source_target_pairs={{0,8},{1,9},{2,10},{3,11},{4,12},{5,13},{6,14},{7,15},{8,16},{9,17... | collective-permute-start | bytes 3538952 | tf_op jit(solution)/shard_map/ppermute | solution.py:33
  124.6 30.1 %copy-start.4 = (bf16[768,768]{1,0:T(8,128)(2,1)}, bf16[768,768]{1,0:T(8,128)(2,1)S(1)}, u32[]{:S(2)}) copy-start(bf16[768,768]{1,0:T(8,128)(2,1)S(1)} %collective-permute-done.12.wb) | copy-start | bytes 3538948
  124.6 36.7 %collective-permute-start.23 = (bf16[512,1536]{1,0:T(8,128)(2,1)}, bf16[512,1536]{1,0:T(8,128)(2,1)S(1)}, u32[]{:S(2)}, u32[]{:S(2)}) collective-permute-start(bf16[512,1536]{1,0:T(8,128)(2,1)} %bitcast.19.refs_16_.refs_17_), channel_id=1, source_target_pairs={{2,0},{3,1},{4,2},{5,3},{6,4},{7,5},{8,6},{9,7},{10,8},{11,9},{12,... | collective-permute-start | bytes 4718600 | tf_op jit(solution)/shard_map/ppermute | solution.py:33
  126.8 35.1 %collective-permute-start.17 = (bf16[512,1536]{1,0:T(8,128)(2,1)S(1)}, bf16[512,1536]{1,0:T(8,128)(2,1)}, u32[]{:S(2)}, u32[]{:S(2)}) collective-permute-start(bf16[512,1536]{1,0:T(8,128)(2,1)S(1)} %bitcast.41), channel_id=1, source_target_pairs={{0,1},{1,0},{2,3},{3,2},{4,5},{5,4},{6,7},{7,6},{8,9},{9,8},{10,11... | collective-permute-start | bytes 4718600 | tf_op jit(solution)/shard_map/ppermute | solution.py:33
  149.0 28.9 %collective-permute-start.2 = (bf16[768,768]{1,0:T(8,128)(2,1)S(1)}, bf16[768,768]{1,0:T(8,128)(2,1)S(1)}, u32[]{:S(2)}, u32[]{:S(2)}) collective-permute-start(bf16[768,768]{1,0:T(8,128)(2,1)S(1)} %bitcast.27), channel_id=1, source_target_pairs={{0,8},{1,9},{2,10},{3,11},{4,12},{5,13},{6,14},{7,15},{8,16},{9,17... | collective-permute-start | bytes 3538952 | tf_op jit(solution)/shard_map/ppermute | solution.py:33
  151.0 28.9 %collective-permute-start.3 = (bf16[768,768]{1,0:T(8,128)(2,1)S(1)}, bf16[768,768]{1,0:T(8,128)(2,1)S(1)}, u32[]{:S(2)}, u32[]{:S(2)}) collective-permute-start(bf16[768,768]{1,0:T(8,128)(2,1)S(1)} %bitcast.28), channel_id=1, source_target_pairs={{0,24},{1,25},{2,26},{3,27},{4,28},{5,29},{6,30},{7,31},{8,0},{9,1... | collective-permute-start | bytes 3538952 | tf_op jit(solution)/shard_map/ppermute | solution.py:33
  161.3 29.4 %collective-permute-start.14 = (bf16[384,768]{1,0:T(8,128)(2,1)}, bf16[384,768]{1,0:T(8,128)(2,1)}, u32[]{:S(2)}, u32[]{:S(2)}) collective-permute-start(bf16[384,768]{1,0:T(8,128)(2,1)} %slice.56), channel_id=1, source_target_pairs={{0,8},{1,9},{2,10},{3,11},{4,12},{5,13},{6,14},{7,15},{8,16},{9,17... | collective-permute-start | bytes 1769480 | tf_op jit(solution)/shard_map/ppermute | solution.py:33
  161.9 66.3 %collective-permute-start.15 = (bf16[384,768]{1,0:T(8,128)(2,1)}, bf16[384,768]{1,0:T(8,128)(2,1)}, u32[]{:S(2)}, u32[]{:S(2)}) collective-permute-start(bf16[384,768]{1,0:T(8,128)(2,1)} %slice.57), channel_id=1, source_target_pairs={{0,24},{1,25},{2,26},{3,27},{4,28},{5,29},{6,30},{7,31},{8,0},{9,1... | collective-permute-start | bytes 1769480 | tf_op jit(solution)/shard_map/ppermute | solution.py:33
  177.9 51.0 %collective-permute-start.10 = (bf16[384,768]{1,0:T(8,128)(2,1)}, bf16[384,768]{1,0:T(8,128)(2,1)}, u32[]{:S(2)}, u32[]{:S(2)}) collective-permute-start(bf16[384,768]{1,0:T(8,128)(2,1)} %slice.54), channel_id=1, source_target_pairs={{0,24},{1,25},{2,26},{3,27},{4,28},{5,29},{6,30},{7,31},{8,0},{9,1... | collective-permute-start | bytes 1769480 | tf_op jit(solution)/shard_map/ppermute | solution.py:33
  180.9 49.7 %collective-permute-start.9 = (bf16[384,768]{1,0:T(8,128)(2,1)}, bf16[384,768]{1,0:T(8,128)(2,1)}, u32[]{:S(2)}, u32[]{:S(2)}) collective-permute-start(bf16[384,768]{1,0:T(8,128)(2,1)} %slice.53), channel_id=1, source_target_pairs={{0,8},{1,9},{2,10},{3,11},{4,12},{5,13},{6,14},{7,15},{8,16},{9,17... | collective-permute-start | bytes 1769480 | tf_op jit(solution)/shard_map/ppermute | solution.py:33
  182.9 48.2 %copy-start.11 = (bf16[512,1536]{1,0:T(8,128)(2,1)S(1)}, bf16[512,1536]{1,0:T(8,128)(2,1)}, u32[]{:S(2)}) copy-start(bf16[512,1536]{1,0:T(8,128)(2,1)} %copy-done.10) | copy-start | bytes 4718596
  185.2 47.2 %copy-start.5 = (bf16[768,768]{1,0:T(8,128)(2,1)S(1)}, bf16[768,768]{1,0:T(8,128)(2,1)}, u32[]{:S(2)}) copy-start(bf16[768,768]{1,0:T(8,128)(2,1)} %copy-done.4) | copy-start | bytes 3538948
  185.2 100.5 %collective-permute-start.18 = (bf16[512,1536]{1,0:T(8,128)(2,1)}, bf16[512,1536]{1,0:T(8,128)(2,1)S(1)}, u32[]{:S(2)}, u32[]{:S(2)}) collective-permute-start(bf16[512,1536]{1,0:T(8,128)(2,1)} %bitcast.37), channel_id=1, source_target_pairs={{0,2},{1,3},{2,4},{3,5},{4,6},{5,7},{6,8},{7,9},{8,10},{9,11},{10,... | collective-permute-start | bytes 4718600 | tf_op jit(solution)/shard_map/ppermute | solution.py:33
  190.7 95.0 %collective-permute-start.19 = (bf16[512,1536]{1,0:T(8,128)(2,1)}, bf16[512,1536]{1,0:T(8,128)(2,1)S(1)}, u32[]{:S(2)}, u32[]{:S(2)}) collective-permute-start(bf16[512,1536]{1,0:T(8,128)(2,1)} %bitcast.38), channel_id=1, source_target_pairs={{2,0},{3,1},{4,2},{5,3},{6,4},{7,5},{8,6},{9,7},{10,8},{11,9},{12,... | collective-permute-start | bytes 4718600 | tf_op jit(solution)/shard_map/ppermute | solution.py:33
  228.2 59.9 %collective-permute-start.21 = (bf16[512,1536]{1,0:T(8,128)(2,1)}, bf16[512,1536]{1,0:T(8,128)(2,1)}, u32[]{:S(2)}, u32[]{:S(2)}) collective-permute-start(bf16[512,1536]{1,0:T(8,128)(2,1)} %bitcast.19.refs_16_.refs_17_), channel_id=1, source_target_pairs={{0,1},{1,0},{2,3},{3,2},{4,5},{5,4},{6,7},{7,6},{8,9},{9,8},{10,11... | collective-permute-start | bytes 4718600 | tf_op jit(solution)/shard_map/ppermute | solution.py:33
  229.0 35.5 %collective-permute-start.4 = (bf16[384,768]{1,0:T(8,128)(2,1)S(1)}, bf16[384,768]{1,0:T(8,128)(2,1)S(1)}, u32[]{:S(2)}, u32[]{:S(2)}) collective-permute-start(bf16[384,768]{1,0:T(8,128)(2,1)S(1)} %slice.50), channel_id=1, source_target_pairs={{0,8},{1,9},{2,10},{3,11},{4,12},{5,13},{6,14},{7,15},{8,16},{9,17... | collective-permute-start | bytes 1769480 | tf_op jit(solution)/shard_map/ppermute | solution.py:33
  230.6 34.6 %collective-permute-start.5 = (bf16[384,768]{1,0:T(8,128)(2,1)S(1)}, bf16[384,768]{1,0:T(8,128)(2,1)S(1)}, u32[]{:S(2)}, u32[]{:S(2)}) collective-permute-start(bf16[384,768]{1,0:T(8,128)(2,1)S(1)} %slice.51), channel_id=1, source_target_pairs={{0,24},{1,25},{2,26},{3,27},{4,28},{5,29},{6,30},{7,31},{8,0},{9,1... | collective-permute-start | bytes 1769480 | tf_op jit(solution)/shard_map/ppermute | solution.py:33
  232.4 34.8 %copy-start.7 = (bf16[768,768]{1,0:T(8,128)(2,1)S(1)}, bf16[768,768]{1,0:T(8,128)(2,1)}, u32[]{:S(2)}) copy-start(bf16[768,768]{1,0:T(8,128)(2,1)} %copy-done.6) | copy-start | bytes 3538948
  242.3 33.8 %copy-start.9 = (bf16[768,768]{1,0:T(8,128)(2,1)S(1)}, bf16[768,768]{1,0:T(8,128)(2,1)}, u32[]{:S(2)}) copy-start(bf16[768,768]{1,0:T(8,128)(2,1)} %copy-done.8) | copy-start | bytes 3538948
  264.5 36.6 %collective-permute-start.24 = (bf16[512,1536]{1,0:T(8,128)(2,1)}, bf16[512,1536]{1,0:T(8,128)(2,1)}, u32[]{:S(2)}, u32[]{:S(2)}) collective-permute-start(bf16[512,1536]{1,0:T(8,128)(2,1)} %broadcast_select_fusion), channel_id=1, source_target_pairs={{0,1},{1,0},{2,3},{3,2},{4,5},{5,4},{6,7},{7,6},{8,9},{9,8},{10,11... | collective-permute-start | bytes 4718600 | tf_op jit(solution)/shard_map/ppermute | solution.py:33
  265.3 55.6 %collective-permute-start.20 = (bf16[512,1536]{1,0:T(8,128)(2,1)}, bf16[512,1536]{1,0:T(8,128)(2,1)}, u32[]{:S(2)}, u32[]{:S(2)}) collective-permute-start(bf16[512,1536]{1,0:T(8,128)(2,1)} %collective-permute-done.17.refs_8_.refs_9_), channel_id=1, source_target_pairs={{0,2},{2,4},{3,1},{4,6},{5,3},{6,8},{7,5},{8,10},{9,7},{10,12},{11... | collective-permute-start | bytes 4718600 | tf_op jit(solution)/shard_map/ppermute | solution.py:33
  276.1 44.8 %copy-start.1 = (bf16[512,768]{1,0:T(8,128)(2,1)S(1)}, bf16[512,768]{1,0:T(8,128)(2,1)}, u32[]{:S(2)}) copy-start(bf16[512,768]{1,0:T(8,128)(2,1)} %copy-done) | copy-start | bytes 2359300
  285.7 35.2 %collective-permute-start.16 = (bf16[512,768]{1,0:T(8,128)(2,1)}, bf16[512,768]{1,0:T(8,128)(2,1)}, u32[]{:S(2)}, u32[]{:S(2)}) collective-permute-start(bf16[512,768]{1,0:T(8,128)(2,1)} %get-tuple-element.18), channel_id=1, source_target_pairs={{0,32},{1,33},{2,34},{3,35},{4,36},{5,37},{6,38},{7,39},{8,40},{9,... | collective-permute-start | bytes 2359304 | tf_op jit(solution)/shard_map/ppermute | solution.py:33
  288.0 32.9 %collective-permute-start.11 = (bf16[512,768]{1,0:T(8,128)(2,1)}, bf16[512,768]{1,0:T(8,128)(2,1)S(1)}, u32[]{:S(2)}, u32[]{:S(2)}) collective-permute-start(bf16[512,768]{1,0:T(8,128)(2,1)} %get-tuple-element.16), channel_id=1, source_target_pairs={{0,32},{1,33},{2,34},{3,35},{4,36},{5,37},{6,38},{7,39},{8,40},{9,... | collective-permute-start | bytes 2359304 | tf_op jit(solution)/shard_map/ppermute | solution.py:33
  288.0 32.9 %collective-permute-start.6 = (bf16[512,768]{1,0:T(8,128)(2,1)}, bf16[512,768]{1,0:T(8,128)(2,1)}, u32[]{:S(2)}, u32[]{:S(2)}) collective-permute-start(bf16[512,768]{1,0:T(8,128)(2,1)} %get-tuple-element.14), channel_id=1, source_target_pairs={{0,32},{1,33},{2,34},{3,35},{4,36},{5,37},{6,38},{7,39},{8,40},{9,... | collective-permute-start | bytes 2359304 | tf_op jit(solution)/shard_map/ppermute | solution.py:33
  (27 other events, 175.2 us)
Sparse Core Ops, SparseCore 0:
  25.8 67.3 all-gather.2
